TPU v7x, 32 devices: a whole 2x2x4 slice. The times are simulated.
32 devices in a mesh: dp: 8 (over y, x, core), tok: 4 (over z).
Axes of the slice: x: 2, y: 2, z: 4, core: 2. Of those that a mesh axis runs over, the one named last changes fastest.
Arguments:
- student_hidden: bfloat16 [16, 1024, 2048], P('dp', 'tok'), may hold values from -48 to 48
- teacher_values: bfloat16 [16, 1024, 4096], P('dp', 'tok'), may hold values from -48 to 48
- value_weight: bfloat16 [2048, 2048], P(None, 'tok'), may hold values from -0.09375 to 0.09375
- value_bias: bfloat16 [1, 2048], P(None, 'tok'), may hold values from -3 to 3
Outputs:
- hidden_grad: bfloat16 [16, 1024, 2048], P('dp', 'tok')
- bias_grad: float32 [2048], P('tok')
All inputs are finite; a program needn't handle non-finite values.
Results may differ from a plain program's by a relative error of at most 0.012.
The roundings to bfloat16 on the way count: a program that leaves them out, or rounds other values in their place, can miss the bound.
Values may be sent and summed in bfloat16 or wider, within the bound.
A program may use at most 64 MiB of HBM per device.

v0:
```python
import math

import jax
import jax.numpy as jnp
from jax import lax
from jax.sharding import PartitionSpec as P

SH = 64
TH = 128


def pair_grads(student_head, teacher_head):
    length = student_head.shape[0]
    block = min(512, length)
    total = jnp.zeros(student_head.shape, jnp.float32)
    contract = (((1,), (1,)), ((), ()))
    for number in range(length // block):
        lower = number * block
        query_student = student_head[lower : lower + block]
        query_teacher = teacher_head[lower : lower + block]
        teacher_scores = lax.dot_general(
            query_teacher, teacher_head, contract, preferred_element_type=jnp.float32
        ) / jnp.sqrt(jnp.float32(TH))
        teacher_prob = jax.nn.softmax(teacher_scores, axis=-1)
        student_scores = lax.dot_general(
            query_student, student_head, contract, preferred_element_type=jnp.float32
        ) / jnp.sqrt(jnp.float32(SH))
        student_prob = jax.nn.softmax(student_scores, axis=-1)
        score_grad = (length * (student_prob - teacher_prob)).astype(jnp.bfloat16)
        total = total.at[lower : lower + block].add(
            jnp.dot(score_grad, student_head, preferred_element_type=jnp.float32)
        )
        total = total + lax.dot_general(
            score_grad, query_student, (((0,), (0,)), ((), ())), preferred_element_type=jnp.float32
        )
    return (total / jnp.sqrt(jnp.float32(SH))).astype(jnp.bfloat16)


def body(student_hidden, teacher_values, value_weight, value_bias):
    seq_count, local_len, width = student_hidden.shape
    rows = student_hidden.reshape(seq_count * local_len, width)
    whole_weight, whole_bias = (
        lax.all_gather(value_weight, "tok", axis=1, tiled=True),
        lax.all_gather(value_bias, "tok", axis=1, tiled=True),
    )
    student_values = (
        jnp.dot(rows, whole_weight, preferred_element_type=jnp.float32)
        + whole_bias.astype(jnp.float32)
    ).astype(jnp.bfloat16)
    value_width = student_values.shape[1]
    student_values = student_values.reshape(seq_count, local_len, value_width)
    student_heads, teacher_heads = (
        lax.all_to_all(student_values, "tok", split_axis=2, concat_axis=1, tiled=True),
        lax.all_to_all(teacher_values, "tok", split_axis=2, concat_axis=1, tiled=True),
    )
    length = student_heads.shape[1]
    head_count = student_heads.shape[2] // SH
    student_items = (
        student_heads.reshape(seq_count, length, head_count, SH)
        .transpose(0, 2, 1, 3)
        .reshape(seq_count * head_count, length, SH)
    )
    teacher_items = (
        teacher_heads.reshape(seq_count, length, head_count, TH)
        .transpose(0, 2, 1, 3)
        .reshape(seq_count * head_count, length, TH)
    )
    grads = lax.map(lambda pair: pair_grads(pair[0], pair[1]), (student_items, teacher_items))
    head_grad = (
        grads.reshape(seq_count, head_count, length, SH)
        .transpose(0, 2, 1, 3)
        .reshape(seq_count, length, head_count * SH)
    )
    token_count = seq_count * length * lax.axis_size("dp")
    local_sum = jnp.sum(head_grad.astype(jnp.float32), axis=(0, 1))
    bias_grad = lax.psum(local_sum, "dp") / math.sqrt(token_count)
    value_grad = lax.all_to_all(head_grad, "tok", split_axis=1, concat_axis=2, tiled=True)
    grad_rows = value_grad.reshape(seq_count * local_len, value_width)
    hidden_grad = lax.dot_general(
        grad_rows, whole_weight, (((1,), (1,)), ((), ())), preferred_element_type=jnp.float32
    )
    hidden_grad = hidden_grad.astype(jnp.bfloat16).reshape(seq_count, local_len, width)
    return (hidden_grad, bias_grad)


def solution(mesh):
    placed = (P("dp", "tok", None), P("dp", "tok", None), P(None, "tok"), P(None, "tok"))
    return jax.shard_map(
        body,
        mesh=mesh,
        in_specs=placed,
        out_specs=(P("dp", "tok", None), P("tok")),
        check_vma=False,
    )
```

profile of v0, /device:TPU:0, one launch (start us, length us, event | category | flops | bytes accessed | tf_op | source)
XLA Modules:
  0.0 587.4 jit_solution(11294621894274342279)
XLA Ops:
  7.9 11.1 %copy.25 = bf16[2,256,4096]{1,0,2:T(2,128)(2,1)} copy(bf16[2,256,4096]{2,1,0:T(8,128)(2,1)} %param.11) | data formatting | bytes 8388608 | tf_op args[1]
  19.0 6.5 %all-to-all-start.1 = ((bf16[2,256,4096]{1,0,2:T(2,128)(2,1)}), bf16[2,256,4096]{1,0,2:T(2,128)(2,1)}, u32[]{:S(2)}, u32[]{:S(2)}) async-start(bf16[2,256,4096]{1,0,2:T(2,128)(2,1)} %copy.25), calls=%async_computation.1 | async-start | bytes 8388608 | tf_op jit(solution)/shard_map/all_to_all | solution.py:54
  25.5 207.9 %all_gather.7 = bf16[1,2048]{1,0:T(2,128)(2,1)S(1)} all-gather(bf16[1,512]{1,0:T(2,128)(2,1)S(1)} %copy-done.2), channel_id=1, replica_groups=mesh['dp'=8,'tok'=4] {'tok'}, dimensions={1}, use_global_device_ids=true | all-gather | bytes 5120 | tf_op jit(solution)/shard_map/all_gather | solution.py:44
  233.4 18.2 %all-gather.2.cloned.1.call-done = bf16[2048,2048]{1,0:T(8,128)(2,1)} async-done(((bf16[2048,512]{1,0:T(8,128)(2,1)}), bf16[2048,2048]{1,0:T(8,128)(2,1)}) %all-gather.2.cloned.1.call-update) | async-done | bytes 8388624 | tf_op jit(solution)/shard_map/all_gather | solution.py:43
  251.6 9.0 %add_convert_fusion = bf16[512,2048]{1,0:T(8,128)(2,1)} fusion(bf16[512,2048]{1,0:T(8,128)(2,1)S(1)} %bitcast.131, bf16[2048,2048]{1,0:T(8,128)(2,1)} %all-gather.2.cloned.1.call-done, f32[2048]{0:T(1024)S(1)} %bitcast.141), kind=kOutput, calls=%fused_computation.47 | convolution fusion | flops 4297064448 | bytes 12591104 | tf_op jit(solution)/shard_map/dot_general | solution.py:47
  260.6 6.1 %copy.22 = bf16[2,256,2048]{1,0,2:T(2,128)(2,1)} copy(bf16[2,256,2048]{2,1,0:T(8,128)(2,1)} %bitcast.140) | data formatting | bytes 4194304 | tf_op jit(solution)/shard_map/reshape | solution.py:51
  266.7 3.8 all-to-all-start
  270.5 11.2 %copy.26 = bf16[2,256,4,1024]{3,1,2,0:T(8,128)(2,1)} copy(bf16[2,256,4,1024]{1,0,3,2:T(2,128)(2,1)} %bitcast.14) | data formatting | bytes 8388608 | tf_op jit(solution)/shard_map/all_to_all | solution.py:54
  281.7 3.3 copy.35
  285.3 2.7 copy.27
  288.0 31.0 %all-to-all-done = bf16[2,256,2048]{1,0,2:T(2,128)(2,1)S(1)} async-done(((bf16[2,256,2048]{1,0,2:T(2,128)(2,1)}), bf16[2,256,2048]{1,0,2:T(2,128)(2,1)S(1)}, u32[]{:S(2)}, u32[]{:S(2)}) %all-to-all-start) | async-done | bytes 2097184 | tf_op jit(solution)/shard_map/all_to_all | solution.py:53
  319.3 1.6 copy.24
  320.9 2.8 reshape.119
  323.7 187.4 %while.15 = (s32[]{:T(128)}, bf16[16,1024,64]{1,2,0:T(8,128)(2,1)}, bf16[16,1024,64]{1,2,0:T(8,128)(2,1)}, bf16[16,1024,128]{2,1,0:T(8,128)(2,1)}, s32[]{:T(128)}, /*index=5*/s32[]{:T(128)}, s32[]{}) while((s32[]{:T(128)}, bf16[16,1024,64]{1,2,0:T(8,128)(2,1)}, bf16[16,1024,64]{1,2,0:T(8,128)(2,1)}, bf16[16,1024,128]{2,1,0:T(8,128)(2,1)}, ...), condition=%wide.region_9.10_spmd, body=%wide.region_0.9_spmd.sunk | while | flops 691269632 | bytes 35039848 | solution.py:68
  325.2 1.6 multiply_reduce_fusion.9
  330.3 1.6 multiply_reduce_fusion.11
  332.8 1.1 multiply_convert_fusion.5
  337.0 1.6 multiply_reduce_fusion.9
  342.0 1.6 multiply_reduce_fusion.11
  344.5 1.1 multiply_convert_fusion.5
  348.7 1.6 multiply_reduce_fusion.9
  353.7 1.6 multiply_reduce_fusion.11
  356.2 1.1 multiply_convert_fusion.5
  360.4 1.6 multiply_reduce_fusion.9
  365.4 1.6 multiply_reduce_fusion.11
  367.9 1.1 multiply_convert_fusion.5
  372.1 1.6 multiply_reduce_fusion.9
  377.2 1.6 multiply_reduce_fusion.11
  379.7 1.1 multiply_convert_fusion.5
  383.8 1.6 multiply_reduce_fusion.9
  388.9 1.6 multiply_reduce_fusion.11
  391.4 1.1 multiply_convert_fusion.5
  395.5 1.6 multiply_reduce_fusion.9
  400.6 1.6 multiply_reduce_fusion.11
  407.2 1.6 multiply_reduce_fusion.9
  412.3 1.6 multiply_reduce_fusion.11
  419.0 1.6 multiply_reduce_fusion.9
  424.0 1.6 multiply_reduce_fusion.11
  426.5 1.1 multiply_convert_fusion.5
  430.7 1.6 multiply_reduce_fusion.9
  435.7 1.6 multiply_reduce_fusion.11
  438.2 1.1 multiply_convert_fusion.5
  442.4 1.6 multiply_reduce_fusion.9
  447.4 1.6 multiply_reduce_fusion.11
  454.1 1.6 multiply_reduce_fusion.9
  459.2 1.6 multiply_reduce_fusion.11
  465.8 1.6 multiply_reduce_fusion.9
  470.9 1.6 multiply_reduce_fusion.11
  477.5 1.6 multiply_reduce_fusion.9
  482.6 1.6 multiply_reduce_fusion.11
  485.1 1.1 multiply_convert_fusion.5
  489.2 1.6 multiply_reduce_fusion.9
  494.3 1.6 multiply_reduce_fusion.11
  496.8 1.1 multiply_convert_fusion.5
  501.0 1.6 multiply_reduce_fusion.9
  506.0 1.6 multiply_reduce_fusion.11
  508.5 1.1 multiply_convert_fusion.5
  511.1 6.2 %copy.29 = bf16[2,1024,512]{2,0,1:T(2,128)(2,1)} copy(bf16[2,1024,512]{1,2,0:T(8,128)(2,1)} %bitcast.20) | data formatting | bytes 4194304 | tf_op jit(solution)/shard_map/reshape | solution.py:72
  517.3 3.6 all-to-all-start.2
  520.9 1.9 convert_reduce_fusion
  522.9 13.8 %psum.7 = f32[512]{0:T(512)S(1)} all-reduce(f32[512]{0:T(512)S(1)} %reduce_sum.64), channel_id=1, replica_groups=mesh['dp'=8,'tok'=4] {'dp'}, use_global_device_ids=true, to_apply=%region_11.12 | all-reduce | flops 512 | bytes 4096 | tf_op jit(solution)/shard_map/psum | solution.py:76
  537.3 31.4 %all-to-all-done.2 = bf16[2,1024,512]{2,0,1:T(2,128)(2,1)S(1)} async-done(((bf16[2,1024,512]{2,0,1:T(2,128)(2,1)}), bf16[2,1024,512]{2,0,1:T(2,128)(2,1)S(1)}, u32[]{:S(2)}, u32[]{:S(2)}) %all-to-all-start.2) | async-done | bytes 2097184 | tf_op jit(solution)/shard_map/all_to_all | solution.py:77
  569.1 1.6 copy.31
  571.3 9.3 %convolution_convert_fusion = bf16[512,2048]{1,0:T(8,128)(2,1)} fusion(bf16[512,2048]{1,0:T(8,128)(2,1)S(1)} %bitcast.139, bf16[2048,2048]{1,0:T(8,128)(2,1)} %all-gather.2.cloned.1.call-done), kind=kOutput, calls=%fused_computation.48 | convolution fusion | flops 4296015872 | bytes 12582912 | tf_op jit(solution)/shard_map/dot_general | solution.py:79
  (230 shorter events, 127.4 us)
Async XLA Ops:
  7.2 244.4 %copy-start = (bf16[2,256,2048]{2,1,0:T(8,128)(2,1)S(1)}, bf16[2,256,2048]{2,1,0:T(8,128)(2,1)}, u32[]{:S(2)}) copy-start(bf16[2,256,2048]{2,1,0:T(8,128)(2,1)} %param.10) | copy-start | bytes 6291460
  7.2 244.4 %all-gather.2.cloned.1.call-start = ((), (), s32[]{:S(2)}) async-start(), calls=%async_computation.3 | async-start | bytes 10485760 | tf_op jit(solution)/shard_map/all_gather | solution.py:43
  19.0 6.5 %copy-start.2 = (bf16[1,512]{1,0:T(2,128)(2,1)S(1)}, bf16[1,512]{1,0:T(2,128)(2,1)}, u32[]{:S(2)}) copy-start(bf16[1,512]{1,0:T(2,128)(2,1)} %param.13) | copy-start | bytes 3076
  19.0 247.7 %all-to-all-start.1 = ((bf16[2,256,4096]{1,0,2:T(2,128)(2,1)}), bf16[2,256,4096]{1,0,2:T(2,128)(2,1)}, u32[]{:S(2)}, u32[]{:S(2)}) async-start(bf16[2,256,4096]{1,0,2:T(2,128)(2,1)} %copy.25), calls=%async_computation.1 | async-start | bytes 8388608 | tf_op jit(solution)/shard_map/all_to_all | solution.py:54
  266.7 52.3 %all-to-all-start = ((bf16[2,256,2048]{1,0,2:T(2,128)(2,1)}), bf16[2,256,2048]{1,0,2:T(2,128)(2,1)S(1)}, u32[]{:S(2)}, u32[]{:S(2)}) async-start(bf16[2,256,2048]{1,0,2:T(2,128)(2,1)} %copy.22), calls=%async_computation | async-start | bytes 4194304 | tf_op jit(solution)/shard_map/all_to_all | solution.py:53
  517.3 51.4 %all-to-all-start.2 = ((bf16[2,1024,512]{2,0,1:T(2,128)(2,1)}), bf16[2,1024,512]{2,0,1:T(2,128)(2,1)S(1)}, u32[]{:S(2)}, u32[]{:S(2)}) async-start(bf16[2,1024,512]{2,0,1:T(2,128)(2,1)} %copy.29), calls=%async_computation.2 | async-start | bytes 4194304 | tf_op jit(solution)/shard_map/all_to_all | solution.py:77
  571.3 9.3 %copy-start.1 = (bf16[2,256,2048]{2,1,0:T(8,128)(2,1)S(1)}, bf16[2,256,2048]{2,1,0:T(8,128)(2,1)}, u32[]{:S(2)}) copy-start(bf16[2,256,2048]{2,1,0:T(8,128)(2,1)} %param.10) | copy-start | bytes 6291460
Sparse Core Ops, SparseCore 0:
  9.6 241.9 all-gather.1
where the time goes:
time: 590 us; the launch traced here: 587 us
  blocking collectives  222 us (38%)
  matrix products  120 us (20%)
  waiting for transfers between devices  81.3 us (14%)
  other arithmetic  68.6 us (12%)
  local copies, waits for them, and re-layouts  66.7 us (11%)
  between operations  14.1 us (2%)
  starting transfers between devices  13.9 us (2%)
    all_gather x1, blocking collectives, body(): lax.all_gather(value_bias, 'tok', axis=1, tiled=True)  208 us
    dot_general x32, matrix products, pair_grads(): lax.dot_general(query_teacher, teacher_head, contract, preferred_element_...  49.6 us
    convert_element_type x32, other arithmetic, pair_grads(): score_grad = (length * (student_prob - teacher_prob)).astype(jnp.bfloat16)  35.7 us
    all_to_all x1, waiting for transfers between devices, body(): lax.all_to_all(head_grad, 'tok', split_axis=1, concat_axis=2, tiled=True)  31.4 us
    all_to_all x1, waiting for transfers between devices, body(): lax.all_to_all(student_values, 'tok', split_axis=2, concat_axis=1, tiled=...  31 us
    reduce_sum x32, other arithmetic, pair_grads(): student_prob = jax.nn.softmax(student_scores, axis=-1)  30.4 us
    dot_general x32, matrix products, pair_grads(): lax.dot_general(score_grad, query_student, (((0,), (0,)), ((), ())), pref...  21.6 us
    all_gather x1, waiting for transfers between devices, body(): lax.all_gather(value_weight, 'tok', axis=1, tiled=True)  18.2 us
  transfers between devices with their start and end apart: 4, of which 3 were waited for; matrix products, arithmetic and copies ran while one was open for 8% of the time, Pallas kernels for 0%

commit v1 on v0

v1 whole, which is shorter than its diff:
```python
import functools
import math

import jax
import jax.numpy as jnp
from jax import lax
from jax.experimental import pallas as pl
from jax.experimental.pallas import tpu as pltpu
from jax.sharding import PartitionSpec as P

SH = 64
TH = 128
PAIR = 128
HEADS_PER = PAIR // SH
LOG2E = math.log2(math.e)


def aligned(index, step):
    return pl.ds(pl.multiple_of(index * step, step), step)


def kernel(
    n_tok, n_dp, seqs, local,
    hidden, teacher, weight, bias,
    out, bias_out,
    w_full, t_full, s_send, s_full, g_buf, vg, bias_all, bsum,
    t_tr, s_tr, s_mask, acc, acc_tr,
    wsend, wrecv, dsend, drecv, csend, crecv, bsend, brecv,
    tsend, trecv, ssend, srecv, gsend, grecv, rsend, rrecv, lsem,
):
    tok = lax.axis_index("tok")
    dp = lax.axis_index("dp")
    width = hidden.shape[1]
    cols = weight.shape[1]
    tcols = teacher.shape[2] // n_tok
    length = n_tok * local
    slice_rows = width // n_dp
    pairs = cols // PAIR
    half = n_dp // 2
    core = lax.rem(dp, 2)
    sibling = dp + 1 - 2 * core

    def tok_at(k):
        return lax.rem(tok + k, n_tok)

    def same_core(k):
        return lax.rem(dp + 2 * k, n_dp)

    def remote(src, dst, send, recv, **where):
        return pltpu.make_async_remote_copy(
            src_ref=src, dst_ref=dst, send_sem=send, recv_sem=recv,
            device_id=where, device_id_type=pl.DeviceIdType.MESH,
        )

    def w_copy(k):
        return remote(
            weight.at[aligned(dp, slice_rows), :],
            w_full.at[aligned(dp, slice_rows), aligned(tok, cols)],
            wsend.at[k], wrecv.at[k], tok=tok_at(k),
        )

    def d_copy(k):
        block = w_full.at[aligned(dp, slice_rows), :]
        return remote(block, block, dsend.at[k], drecv.at[k], dp=same_core(k))

    def c_copy(k):
        owner = lax.rem(dp - 2 * k + n_dp, n_dp)
        block = w_full.at[aligned(owner, slice_rows), :]
        return remote(block, block, csend.at[k], crecv.at[k], dp=sibling)

    def b_copy(k):
        return remote(bias_all.at[tok], bias_all.at[tok], bsend.at[k], brecv.at[k], tok=tok_at(k))

    def t_copy(s, k):
        return remote(
            teacher.at[s, :, aligned(tok_at(k), tcols)],
            t_full.at[s, aligned(tok, local), :],
            tsend.at[s, k], trecv.at[s, k], tok=tok_at(k),
        )

    def s_copy(s, k):
        return remote(
            s_send.at[k, s], s_full.at[s, aligned(tok, local), :],
            ssend.at[s, k], srecv.at[s, k], tok=tok_at(k),
        )

    def g_copy(s, j, k):
        return remote(
            g_buf.at[s, aligned(tok_at(k), local), aligned(j, PAIR)],
            vg.at[s, :, aligned(tok * pairs + j, PAIR)],
            gsend.at[s, j, k], grecv.at[s, j, k], tok=tok_at(k),
        )

    def r_copy(k):
        return remote(bsum.at[dp], bsum.at[dp], rsend.at[k], rrecv.at[k], dp=lax.rem(dp + k, n_dp))

    def own_w():
        return pltpu.make_async_copy(
            weight.at[aligned(dp, slice_rows), :],
            w_full.at[aligned(dp, slice_rows), aligned(tok, cols)], lsem.at[0],
        )

    def own_t(s):
        return pltpu.make_async_copy(
            teacher.at[s, :, aligned(tok, tcols)], t_full.at[s, aligned(tok, local), :], lsem.at[1 + s]
        )

    barrier = pltpu.get_barrier_semaphore()
    for k in range(1, n_tok):
        pl.semaphore_signal(barrier, inc=1, device_id={"tok": tok_at(k)}, device_id_type=pl.DeviceIdType.MESH)
    for k in range(1, n_dp):
        pl.semaphore_signal(
            barrier, inc=1, device_id={"dp": lax.rem(dp + k, n_dp)}, device_id_type=pl.DeviceIdType.MESH
        )
    bias_all[tok] = bias[...]
    own_w().start()
    for s in range(seqs):
        own_t(s).start()
    pl.semaphore_wait(barrier, n_tok + n_dp - 2)

    for k in range(1, n_tok):
        w_copy(k).start()
        b_copy(k).start()
    own_w().wait()
    for k in range(1, n_tok):
        w_copy(k).wait_recv()
    for k in range(1, half):
        d_copy(k).start()
    c_copy(0).start()
    for s in range(seqs):
        for k in range(1, n_tok):
            t_copy(s, k).start()
    for k in range(1, half):
        d_copy(k).wait_recv()
        c_copy(k).start()
    for k in range(half):
        c_copy(k).wait_recv()
    for k in range(1, n_tok):
        b_copy(k).wait_recv()

    def project(step, carry):
        k = lax.rem(step + 1, n_tok)
        p = tok_at(k)
        values = jnp.dot(hidden[...], w_full[:, aligned(p, cols)], preferred_element_type=jnp.float32)
        values = (values + bias_all[p][0:1, :]).astype(jnp.bfloat16)

        @pl.when(k > 0)
        def _():
            for s in range(seqs):
                s_send[k, s] = values[s * local : (s + 1) * local]
                s_copy(s, k).start()

        @pl.when(k == 0)
        def _():
            for s in range(seqs):
                s_full[s, aligned(tok, local), :] = values[s * local : (s + 1) * local]

        return carry

    lax.fori_loop(0, n_tok, project, 0)

    block = min(256, length)
    lane_head = lax.broadcasted_iota(jnp.int32, (length, PAIR), 1) // SH
    t_scale = LOG2E / math.sqrt(TH)
    s_scale = LOG2E / math.sqrt(SH)

    def softmax_terms(scores, scale):
        top = jnp.max(scores, axis=1, keepdims=True)
        terms = jnp.exp2((scores - top) * scale)
        return terms, length / jnp.sum(terms, axis=1, keepdims=True)

    def unit(s, j):
        values = s_full[s, :, aligned(j, PAIR)]
        s_tr[...] = values.T
        for h in range(HEADS_PER):
            s_mask[h] = jnp.where(lane_head == h, values, jnp.zeros_like(values))
            t_tr[h] = t_full[s, :, aligned(j * HEADS_PER + h, TH)].T
        acc_tr[...] = jnp.zeros_like(acc_tr)

        def query(i, carry):
            rows = aligned(i, block)
            total = None
            for h in range(HEADS_PER):
                t_scores = jnp.dot(
                    t_full[s, rows, aligned(j * HEADS_PER + h, TH)], t_tr[h], preferred_element_type=jnp.float32
                )
                s_scores = jnp.dot(s_mask[h, rows, :], s_tr[...], preferred_element_type=jnp.float32)
                t_terms, t_norm = softmax_terms(t_scores, t_scale)
                s_terms, s_norm = softmax_terms(s_scores, s_scale)
                grad = (s_terms * s_norm - t_terms * t_norm).astype(jnp.bfloat16)
                part = jnp.dot(grad, s_mask[h], preferred_element_type=jnp.float32)
                total = part if total is None else total + part
                acc_tr[h * SH : (h + 1) * SH, :] += jnp.dot(
                    s_tr[h * SH : (h + 1) * SH, rows], grad, preferred_element_type=jnp.float32
                )
            acc[rows, :] = total
            return carry

        lax.fori_loop(0, length // block, query, 0)
        result = ((acc[...] + acc_tr[...].T) * (1.0 / math.sqrt(SH))).astype(jnp.bfloat16)
        g_buf[s, :, aligned(j, PAIR)] = result
        part = jnp.sum(result.astype(jnp.float32).reshape(length // 8, 8, PAIR), axis=0)
        bsum[dp, :, aligned(j, PAIR)] += part
        vg[s, :, aligned(tok * pairs + j, PAIR)] = g_buf[s, aligned(tok, local), aligned(j, PAIR)]

    bsum[dp] = jnp.zeros_like(bias)

    def sequence(s, carry):
        pltpu.make_async_copy(
            teacher.at[s, :, aligned(tok, tcols)], t_full.at[s, aligned(tok, local), :], lsem.at[1 + s]
        ).wait()
        for k in range(1, n_tok):
            t_copy(s, k).wait_recv()
        for k in range(1, n_tok):
            s_copy(s, k).wait_recv()

        def pair(j, inner):
            unit(s, j)
            for k in range(1, n_tok):
                g_copy(s, j, k).start()
            return inner

        lax.fori_loop(0, pairs, pair, 0)
        return carry

    lax.fori_loop(0, seqs, sequence, 0)

    for k in range(1, n_dp):
        r_copy(k).start()

    out_block = min(256, width)

    def finish(s, carry):
        def arrive(j, inner):
            for k in range(1, n_tok):
                g_copy(s, j, k).wait_recv()
            return inner

        lax.fori_loop(0, pairs, arrive, 0)

        def columns(b, inner):
            out[s, :, aligned(b, out_block)] = lax.dot_general(
                vg[s], w_full[aligned(b, out_block), :], (((1,), (1,)), ((), ())),
                preferred_element_type=jnp.float32,
            ).astype(jnp.bfloat16)
            return inner

        lax.fori_loop(0, width // out_block, columns, 0)
        return carry

    lax.fori_loop(0, seqs, finish, 0)

    for k in range(1, n_dp):
        r_copy(k).wait_recv()
    total = bsum[0]
    for d in range(1, n_dp):
        total = total + bsum[d]
    total = jnp.sum(total, axis=0, keepdims=True) * (1.0 / math.sqrt(seqs * n_dp * length))
    bias_out[...] = jnp.broadcast_to(total, bias_out.shape)

    for k in range(1, n_tok):
        w_copy(k).wait_send()
        b_copy(k).wait_send()
        for s in range(seqs):
            t_copy(s, k).wait_send()
            s_copy(s, k).wait_send()

    def sent(j, carry):
        for s in range(seqs):
            for k in range(1, n_tok):
                g_copy(s, j, k).wait_send()
        return carry

    lax.fori_loop(0, pairs, sent, 0)
    for k in range(1, half):
        d_copy(k).wait_send()
    for k in range(half):
        c_copy(k).wait_send()
    for k in range(1, n_dp):
        r_copy(k).wait_send()


def body(student_hidden, teacher_values, value_weight, value_bias):
    seqs, local, width = student_hidden.shape
    n_tok = lax.axis_size("tok")
    n_dp = lax.axis_size("dp")
    cols = value_weight.shape[1]
    length = n_tok * local
    tcols = teacher_values.shape[2] // n_tok
    pairs = cols // PAIR
    rows = student_hidden.reshape(seqs * local, width)
    bias = jnp.broadcast_to(value_bias.astype(jnp.float32), (8, cols))
    dma = pltpu.SemaphoreType.DMA
    half = n_dp // 2
    bf16, f32 = jnp.bfloat16, jnp.float32
    hidden_grad, bias_grad = pl.pallas_call(
        functools.partial(kernel, n_tok, n_dp, seqs, local),
        out_shape=(
            jax.ShapeDtypeStruct((seqs, local, width), bf16),
            jax.ShapeDtypeStruct((8, cols), f32),
        ),
        in_specs=[
            pl.BlockSpec(memory_space=pltpu.VMEM),
            pl.BlockSpec(memory_space=pl.ANY),
            pl.BlockSpec(memory_space=pl.ANY),
            pl.BlockSpec(memory_space=pltpu.VMEM),
        ],
        out_specs=(pl.BlockSpec(memory_space=pltpu.VMEM),) * 2,
        scratch_shapes=[
            pltpu.VMEM((width, n_tok * cols), bf16),
            pltpu.VMEM((seqs, length, tcols), bf16),
            pltpu.VMEM((n_tok, seqs, local, cols), bf16),
            pltpu.VMEM((seqs, length, cols), bf16),
            pltpu.VMEM((seqs, length, cols), bf16),
            pltpu.VMEM((seqs, local, n_tok * cols), bf16),
            pltpu.VMEM((n_tok, 8, cols), f32),
            pltpu.VMEM((n_dp, 8, cols), f32),
            pltpu.VMEM((HEADS_PER, TH, length), bf16),
            pltpu.VMEM((PAIR, length), bf16),
            pltpu.VMEM((HEADS_PER, length, PAIR), bf16),
            pltpu.VMEM((length, PAIR), f32),
            pltpu.VMEM((PAIR, length), f32),
            dma((n_tok,)), dma((n_tok,)),
            dma((half,)), dma((half,)),
            dma((half,)), dma((half,)),
            dma((n_tok,)), dma((n_tok,)),
            dma((seqs, n_tok)), dma((seqs, n_tok)),
            dma((seqs, n_tok)), dma((seqs, n_tok)),
            dma((seqs, pairs, n_tok)), dma((seqs, pairs, n_tok)),
            dma((n_dp,)), dma((n_dp,)),
            dma((1 + seqs,)),
        ],
        compiler_params=pltpu.CompilerParams(
            collective_id=0, has_side_effects=True, vmem_limit_bytes=56 * 2**20
        ),
    )(rows, teacher_values, value_weight, bias)
    return hidden_grad, bias_grad[0]


def solution(mesh):
    placed = (P("dp", "tok", None), P("dp", "tok", None), P(None, "tok"), P(None, "tok"))
    return jax.shard_map(
        body,
        mesh=mesh,
        in_specs=placed,
        out_specs=(P("dp", "tok", None), P("tok")),
        check_vma=False,
    )
```

time: 590 us -> 255 us (0.43)
  Pallas kernels: 0 us -> 249 us
  blocking collectives: 222 us -> 0 us
  matrix products: 120 us -> 0 us
  waiting for transfers between devices: 81.3 us -> 0 us
  other arithmetic: 68.6 us -> 0.69 us
  local copies, waits for them, and re-layouts: 66.7 us -> 5.06 us
  starting transfers between devices: 13.9 us -> 0 us
  between operations: 14.1 us -> 0.64 us
    pallas_call x0 -> x1, Pallas kernels: none -> 249 us  [body(): pl.pallas_call(functools.partial(kernel, n_tok, n_dp, seqs, local), out_s...]
    all_gather x1 -> x0, blocking collectives: 208 us -> none  [body(): lax.all_gather(value_bias, 'tok', axis=1, tiled=True)]
    dot_general x130 -> x0, matrix products: 120 us -> none  [the longest x32 49.6 us: pair_grads(): lax.dot_general(query_teacher, teacher_head, contract, preferred_element_...]
    all_to_all x3 -> x0, waiting for transfers between devices: 62.4 us -> none  [the longest x1 31.4 us: body(): lax.all_to_all(head_grad, 'tok', split_axis=1, concat_axis=2, tiled=True)]
    convert_element_type x32 -> x0, other arithmetic: 35.7 us -> none  [pair_grads(): score_grad = (length * (student_prob - teacher_prob)).astype(jnp.bfloat16)]
    reduce_sum x33 -> x0, other arithmetic: 32.3 us -> none  [the longest x32 30.4 us: pair_grads(): student_prob = jax.nn.softmax(student_scores, axis=-1)]
    all_gather x1 -> x0, waiting for transfers between devices: 18.2 us -> none  [body(): lax.all_gather(value_weight, 'tok', axis=1, tiled=True)]
    reshape x3 -> x0, local copies, waits for them, and re-layouts: 15.1 us -> none  [the longest x1 6.16 us: body(): head_grad = grads.reshape(seq_count, head_count, length, SH).transpose(0,...]
  transfers between devices with their start and end apart: 4 -> 0, of which waited for: 3 -> 0; matrix products, arithmetic and copies ran while one was open for 8% -> 0% of each run, Pallas kernels for 0% -> 0%
where the time goes in v1:
time: 255 us
  Pallas kernels  249 us (98%)
  local copies, waits for them, and re-layouts  5.06 us (2%)
    pallas_call x1, Pallas kernels, body(): pl.pallas_call(functools.partial(kernel, n_tok, n_dp, seqs, local), out_s...  249 us

profile of v1, /device:TPU:0, one launch (start us, length us, event | category | flops | bytes accessed | tf_op | source)
XLA Modules:
  0.0 255.0 jit_solution(18136037128879282527)
XLA Ops:
  0.6 0.7 broadcast_in_dim.13
  1.3 0.6 broadcast_in_dim.12.bias
  1.9 248.6 %shard_map.59 = (bf16[2,256,2048]{2,1,0:T(8,128)(2,1)}, f32[8,512]{1,0:T(8,128)}) custom-call(bf16[512,2048]{1,0:T(8,128)(2,1)} %bitcast.3, bf16[2,256,4096]{2,1,0:T(8,128)(2,1)} %teacher.1, bf16[2048,512]{1,0:T(8,128)(2,1)} %weight.1, f32[8,512]{1,0:T(8,128)} %broadcast_in_dim.12.bias), custom_call_target="tpu_custom_call" | custom-call | tf_op jit(solution)/shard_map/pallas_call | solution.py:296
  250.5 1.3 slice.3
  251.8 3.2 %copy.7 = bf16[2,256,2048]{2,1,0:T(8,128)(2,1)} copy(bf16[2,256,2048]{2,1,0:T(8,128)(2,1)} %get-tuple-element.8) | data formatting | bytes 4194304

commit v2 on v1

--- a/solution.py
+++ b/solution.py
@@ -52,21 +52,22 @@
             device_id=where, device_id_type=pl.DeviceIdType.MESH,
         )
 
-    def w_copy(k):
+    def w_block(owner, q):
+        return w_full.at[aligned(owner, slice_rows), aligned(q, cols)]
+
+    def w_copy(q, step):
+        src = weight.at[aligned(dp, slice_rows), :] if q is tok else w_block(dp, q)
         return remote(
-            weight.at[aligned(dp, slice_rows), :],
-            w_full.at[aligned(dp, slice_rows), aligned(tok, cols)],
-            wsend.at[k], wrecv.at[k], tok=tok_at(k),
-        )
-
-    def d_copy(k):
-        block = w_full.at[aligned(dp, slice_rows), :]
-        return remote(block, block, dsend.at[k], drecv.at[k], dp=same_core(k))
-
-    def c_copy(k):
-        owner = lax.rem(dp - 2 * k + n_dp, n_dp)
-        block = w_full.at[aligned(owner, slice_rows), :]
-        return remote(block, block, csend.at[k], crecv.at[k], dp=sibling)
+            src, w_block(dp, q), wsend.at[(step + 1) // 2, q], wrecv.at[q], tok=lax.rem(tok + step + n_tok, n_tok)
+        )
+
+    def d_copy(q, m):
+        block = w_block(dp, q)
+        return remote(block, block, dsend.at[q, m], drecv.at[q, m], dp=same_core(m))
+
+    def c_copy(q, m):
+        block = w_block(lax.rem(dp - 2 * m + n_dp, n_dp), q)
+        return remote(block, block, csend.at[q, m], crecv.at[q, m], dp=sibling)
 
     def b_copy(k):
         return remote(bias_all.at[tok], bias_all.at[tok], bsend.at[k], brecv.at[k], tok=tok_at(k))
@@ -95,10 +96,7 @@
         return remote(bsum.at[dp], bsum.at[dp], rsend.at[k], rrecv.at[k], dp=lax.rem(dp + k, n_dp))
 
     def own_w():
-        return pltpu.make_async_copy(
-            weight.at[aligned(dp, slice_rows), :],
-            w_full.at[aligned(dp, slice_rows), aligned(tok, cols)], lsem.at[0],
-        )
+        return pltpu.make_async_copy(weight, w_full.at[:, aligned(tok, cols)], lsem.at[0])
 
     def own_t(s):
         return pltpu.make_async_copy(
@@ -118,46 +116,91 @@
         own_t(s).start()
     pl.semaphore_wait(barrier, n_tok + n_dp - 2)
 
+    has_left, has_right = tok > 0, tok < n_tok - 1
+
+    def pass_left(q):
+        @pl.when(has_left)
+        def _():
+            w_copy(q, -1).start()
+
+    def pass_right(q):
+        @pl.when(has_right)
+        def _():
+            w_copy(q, 1).start()
+
+    pass_left(tok)
+    pass_right(tok)
     for k in range(1, n_tok):
-        w_copy(k).start()
         b_copy(k).start()
-    own_w().wait()
-    for k in range(1, n_tok):
-        w_copy(k).wait_recv()
-    for k in range(1, half):
-        d_copy(k).start()
-    c_copy(0).start()
-    for s in range(seqs):
+
+    def spread(q):
+        for m in range(1, half):
+            d_copy(q, m).start()
+        c_copy(q, 0).start()
+
+    def arrived(dist):
+        @pl.when(tok - dist >= 0)
+        def _():
+            q = tok - dist
+            w_copy(q, 1).wait_recv()
+            pass_right(q)
+            spread(q)
+
+        @pl.when(tok + dist < n_tok)
+        def _():
+            q = tok + dist
+            w_copy(q, -1).wait_recv()
+            pass_left(q)
+            spread(q)
+
+    def start_teacher(s):
         for k in range(1, n_tok):
             t_copy(s, k).start()
-    for k in range(1, half):
-        d_copy(k).wait_recv()
-        c_copy(k).start()
-    for k in range(half):
-        c_copy(k).wait_recv()
+
+    def project(s, k):
+        p = tok_at(k)
+        values = jnp.dot(
+            hidden[s * local : (s + 1) * local, :], w_full[:, aligned(p, cols)], preferred_element_type=jnp.float32
+        )
+        return (values + bias_all[p][0:1, :]).astype(jnp.bfloat16)
+
+    arrived(1)
+    start_teacher(0)
+    for dist in range(2, n_tok):
+        arrived(dist)
+    own_w().wait()
+    for s in range(seqs):
+        s_full[s, aligned(tok, local), :] = project(s, 0)
+
+    def block_at(k):
+        return lax.rem(tok - k + n_tok, n_tok)
+
+    def forward(k, carry):
+        for m in range(1, half):
+            d_copy(block_at(k), m).wait_recv()
+            c_copy(block_at(k), m).start()
+        return carry
+
+    lax.fori_loop(1, n_tok, forward, 0)
     for k in range(1, n_tok):
         b_copy(k).wait_recv()
 
-    def project(step, carry):
-        k = lax.rem(step + 1, n_tok)
-        p = tok_at(k)
-        values = jnp.dot(hidden[...], w_full[:, aligned(p, cols)], preferred_element_type=jnp.float32)
-        values = (values + bias_all[p][0:1, :]).astype(jnp.bfloat16)
-
-        @pl.when(k > 0)
-        def _():
-            for s in range(seqs):
-                s_send[k, s] = values[s * local : (s + 1) * local]
-                s_copy(s, k).start()
-
-        @pl.when(k == 0)
-        def _():
-            for s in range(seqs):
-                s_full[s, aligned(tok, local), :] = values[s * local : (s + 1) * local]
-
-        return carry
-
-    lax.fori_loop(0, n_tok, project, 0)
+    def first(k, carry):
+        for m in range(half):
+            c_copy(block_at(k), m).wait_recv()
+        s_send[n_tok - k, 0] = project(0, n_tok - k)
+        s_copy(0, n_tok - k).start()
+        return carry
+
+    lax.fori_loop(1, n_tok, first, 0)
+    for s in range(1, seqs):
+        start_teacher(s)
+
+        def later(k, carry):
+            s_send[k, s] = project(s, k)
+            return carry
+
+        lax.fori_loop(1, n_tok, later, 0)
 
     block = min(256, length)
     lane_head = lax.broadcasted_iota(jnp.int32, (length, PAIR), 1) // SH
@@ -214,6 +257,11 @@
         for k in range(1, n_tok):
             s_copy(s, k).wait_recv()
 
+        @pl.when(s + 1 < seqs)
+        def _():
+            for k in range(1, n_tok):
+                s_copy(s + 1, k).start()
+
         def pair(j, inner):
             unit(s, j)
             for k in range(1, n_tok):
@@ -259,12 +307,20 @@
     bias_out[...] = jnp.broadcast_to(total, bias_out.shape)
 
     for k in range(1, n_tok):
-        w_copy(k).wait_send()
         b_copy(k).wait_send()
         for s in range(seqs):
             t_copy(s, k).wait_send()
             s_copy(s, k).wait_send()
 
+    for q in range(n_tok):
+        @pl.when((tok <= q) & has_left)
+        def _():
+            w_copy(q, -1).wait_send()
+
+        @pl.when((tok >= q) & has_right)
+        def _():
+            w_copy(q, 1).wait_send()
+
     def sent(j, carry):
         for s in range(seqs):
             for k in range(1, n_tok):
@@ -272,10 +328,14 @@
         return carry
 
     lax.fori_loop(0, pairs, sent, 0)
-    for k in range(1, half):
-        d_copy(k).wait_send()
-    for k in range(half):
-        c_copy(k).wait_send()
+    def passed(k, carry):
+        for m in range(1, half):
+            d_copy(block_at(k), m).wait_send()
+        for m in range(half):
+            c_copy(block_at(k), m).wait_send()
+        return carry
+
+    lax.fori_loop(1, n_tok, passed, 0)
     for k in range(1, n_dp):
         r_copy(k).wait_send()
 
@@ -320,9 +380,9 @@
             pltpu.VMEM((HEADS_PER, length, PAIR), bf16),
             pltpu.VMEM((length, PAIR), f32),
             pltpu.VMEM((PAIR, length), f32),
-            dma((n_tok,)), dma((n_tok,)),
-            dma((half,)), dma((half,)),
-            dma((half,)), dma((half,)),
+            dma((2, n_tok)), dma((n_tok,)),
+            dma((n_tok, half)), dma((n_tok, half)),
+            dma((n_tok, half)), dma((n_tok, half)),
             dma((n_tok,)), dma((n_tok,)),
             dma((seqs, n_tok)), dma((seqs, n_tok)),
             dma((seqs, n_tok)), dma((seqs, n_tok)),

time: 255 us -> 222 us (0.87)
  Pallas kernels: 249 us -> 215 us
    pallas_call x1, Pallas kernels: 249 us -> 215 us  [body(): pl.pallas_call(functools.partial(kernel, n_tok, n_dp, seqs, local), out_s...]
where the time goes in v2:
time: 222 us; the launch traced here: 221 us
  Pallas kernels  215 us (97%)
  local copies, waits for them, and re-layouts  5.06 us (2%)
    pallas_call x1, Pallas kernels, body(): pl.pallas_call(functools.partial(kernel, n_tok, n_dp, seqs, local), out_s...  215 us

profile of v2, /device:TPU:0, one launch (start us, length us, event | category | flops | bytes accessed | tf_op | source)
XLA Modules:
  0.0 221.0 jit_solution(9865275139516197895)
XLA Ops:
  0.6 0.7 broadcast_in_dim.13
  1.3 0.6 broadcast_in_dim.12.bias
  1.9 214.6 %shard_map.59 = (bf16[2,256,2048]{2,1,0:T(8,128)(2,1)}, f32[8,512]{1,0:T(8,128)}) custom-call(bf16[512,2048]{1,0:T(8,128)(2,1)} %bitcast.3, bf16[2,256,4096]{2,1,0:T(8,128)(2,1)} %teacher.1, bf16[2048,512]{1,0:T(8,128)(2,1)} %weight.1, f32[8,512]{1,0:T(8,128)} %broadcast_in_dim.12.bias), custom_call_target="tpu_custom_call" | custom-call | tf_op jit(solution)/shard_map/pallas_call | solution.py:356
  216.5 1.3 slice.3
  217.8 3.2 %copy.7 = bf16[2,256,2048]{2,1,0:T(8,128)(2,1)} copy(bf16[2,256,2048]{2,1,0:T(8,128)(2,1)} %get-tuple-element.8) | data formatting | bytes 4194304

commit v3 on v2

--- a/solution.py
+++ b/solution.py
@@ -168,6 +168,8 @@
     start_teacher(0)
     for dist in range(2, n_tok):
         arrived(dist)
+    for s in range(1, seqs):
+        start_teacher(s)
     own_w().wait()
     for s in range(seqs):
         s_full[s, aligned(tok, local), :] = project(s, 0)
@@ -194,8 +196,6 @@
 
     lax.fori_loop(1, n_tok, first, 0)
     for s in range(1, seqs):
-        start_teacher(s)
-
         def later(k, carry):
             s_send[k, s] = project(s, k)
             return carry

time: 222 us -> 236 us (1.063)
  Pallas kernels: 215 us -> 230 us
    pallas_call x1, Pallas kernels: 215 us -> 230 us  [body(): pl.pallas_call(functools.partial(kernel, n_tok, n_dp, seqs, local), out_s...]
where the time goes in v3:
time: 236 us
  Pallas kernels  230 us (97%)
  local copies, waits for them, and re-layouts  5.06 us (2%)
    pallas_call x1, Pallas kernels, body(): pl.pallas_call(functools.partial(kernel, n_tok, n_dp, seqs, local), out_s...  230 us

profile of v3, /device:TPU:0, one launch (start us, length us, event | category | flops | bytes accessed | tf_op | source)
XLA Modules:
  0.0 236.0 jit_solution(13474359961896604166)
XLA Ops:
  0.6 0.7 broadcast_in_dim.13
  1.3 0.6 broadcast_in_dim.12.bias
  1.9 229.6 %shard_map.59 = (bf16[2,256,2048]{2,1,0:T(8,128)(2,1)}, f32[8,512]{1,0:T(8,128)}) custom-call(bf16[512,2048]{1,0:T(8,128)(2,1)} %bitcast.3, bf16[2,256,4096]{2,1,0:T(8,128)(2,1)} %teacher.1, bf16[2048,512]{1,0:T(8,128)(2,1)} %weight.1, f32[8,512]{1,0:T(8,128)} %broadcast_in_dim.12.bias), custom_call_target="tpu_custom_call" | custom-call | tf_op jit(solution)/shard_map/pallas_call | solution.py:356
  231.5 1.3 slice.3
  232.8 3.2 %copy.7 = bf16[2,256,2048]{2,1,0:T(8,128)(2,1)} copy(bf16[2,256,2048]{2,1,0:T(8,128)(2,1)} %get-tuple-element.8) | data formatting | bytes 4194304
